TPU v7x, 32 devices: a whole 2x2x4 slice. The times are simulated.
32 devices in a mesh: col: 8 (over z, y), row: 4 (over x, core).
Axes of the slice: x: 2, y: 2, z: 4, core: 2. Of those that a mesh axis runs over, the one named last changes fastest.
Arguments:
- r_slab: float32 [1024, 2048], P('row', 'col'), may hold values from -4 to 8, as said below
- arc_rows: float32 [4096, 2048], P('row', 'col'), may hold values from -6 to 6
- arc_blocks: int32 [32, 8], P('row', 'col'), may hold values 0 or 1
Outputs:
- r_updated: float32 [1024, 2048], P('row', 'col')
Inputs may be any that keep to these rules, and one draw needn't show every extreme that they name: r_slab is zero wherever an entry's global column index is below its row index, and its diagonal is positive.
All inputs are finite; a program needn't handle non-finite values. No bound on the sum of `arc_blocks` on one device may be relied on, other than what follows from the above.
Results may differ from a plain program's by a relative error of at most 0.000098.
Values sent between devices are 32-bit elements; how exact they have to be, the bound alone decides.
No kernel may reach another device: no remote copies, remote signals or barrier semaphores. Data moves between devices by JAX's collectives and lax.ppermute only.
A program may use at most 64 MiB of HBM per device.

v0:
```python
import jax
import jax.numpy as jnp
from jax import lax
from jax.sharding import PartitionSpec as P

B = 256
P_SIZE = 4
ARC_ROWS = 128


def spread(value, axis, source):
    kept = jnp.where(lax.axis_index(axis) == source, value, 0).astype(value.dtype)
    return lax.psum(kept, axis)


def inner_dot(left, right):
    return jnp.dot(left.T, right, precision=lax.Precision.HIGHEST)


def upper_keep(row_start, height, columns, col_index, n_col):
    row_ids = row_start + lax.broadcasted_iota(jnp.int32, (height, columns), 0)
    col_ids = lax.broadcasted_iota(jnp.int32, (height, columns), 1)
    global_col = (col_ids // B * n_col + col_index) * B + col_ids % B
    return global_col >= row_ids


def on_device(r_slab, arc_rows, arc_blocks):
    n_col = lax.axis_size("col")
    col_index = lax.axis_index("col")
    row_index = lax.axis_index("row")
    n_arcs, blocks_here = arc_blocks.shape
    columns = arc_rows.shape[1]
    live = arc_blocks.astype(jnp.float32)
    masked = (arc_rows.reshape(n_arcs, ARC_ROWS, blocks_here, B) * live[:, None, :, None]).reshape(
        arc_rows.shape
    )
    stacked = jnp.concatenate([r_slab, masked], axis=0)
    pieces = []
    for panel_id in range(P_SIZE):
        owner = panel_id % n_col
        pieces.append(spread(stacked, "col", owner))
    panels = jnp.concatenate(pieces, axis=1)
    gram, cross = lax.psum((inner_dot(panels, panels), inner_dot(panels, stacked)), "row")
    lower = jnp.linalg.cholesky(gram)
    factor = jax.scipy.linalg.solve_triangular(lower, cross, lower=True)
    mine = lax.dynamic_slice_in_dim(factor, row_index * B, B, 0)
    keep = upper_keep(row_index * B, B, columns, col_index, n_col)
    result = jnp.where(keep, mine, jnp.zeros_like(mine))
    return result


def solution(mesh):
    return jax.shard_map(
        on_device,
        mesh=mesh,
        in_specs=(P("row", "col"), P("row", "col"), P("row", "col")),
        out_specs=P("row", "col"),
        check_vma=False,
    )
```

profile of v0, /device:TPU:9, one launch (start us, length us, event | category | flops | bytes accessed | tf_op | source)
XLA Modules:
  0.0 674.1 jit_solution(3496541189155743681)
XLA Ops:
  8.7 3.4 broadcast_select_fusion
  12.2 184.3 %all-reduce.6.cloned.1.call-done = (f32[1280,256]{1,0:T(8,128)}, f32[1280,256]{1,0:T(8,128)}, f32[1280,256]{1,0:T(8,128)}, f32[1280,256]{1,0:T(8,128)}) async-done(((f32[1280,256]{1,0:T(8,128)}, f32[1280,256]{1,0:T(8,128)}, f32[1280,256]{1,0:T(8,128)}, f32[1280,256]{1,0:T(8,128)}), (f32[1280,256]{1,0:T(8,128)}, f32[1280,256]{1,0:T(8,128)}, f32[1280,256]{1,0:T(8,128)}, ...) | async-done | bytes 5242896 | tf_op jit(solution)/shard_map/psum | solution.py:13
  196.5 1.7 constant_dynamic-update-slice_fusion.3
  198.1 1.5 constant_dynamic-update-slice_fusion.2
  200.1 18.7 %fusion.66 = f32[1024,1024]{0,1:T(8,128)} fusion(f32[1280,1024]{1,0:T(8,128)S(1)} %constant_dynamic-update-slice_fusion), kind=kOutput, calls=%fused_computation.180 | convolution fusion | flops 16106127360 | bytes 9437184 | tf_op jit(solution)/shard_map/dot_general | solution.py:17
  218.8 9.5 %fusion.25 = f32[1024,256]{1,0:T(8,128)} fusion(f32[1280,1024]{1,0:T(8,128)S(1)} %constant_dynamic-update-slice_fusion, f32[1024,256]{1,0:T(8,128)S(1)} %broadcast_multiply_fusion, f32[256,256]{1,0:T(8,128)S(1)} %copy-done.3), kind=kOutput, calls=%fused_computation.57 | convolution fusion | flops 4026859520 | bytes 7602176 | tf_op jit(solution)/shard_map/dot_general | solution.py:17
  228.4 103.5 %all-reduce.8.cloned.1.call-done = (f32[1024,256]{1,0:T(8,128)}, f32[1024,1024]{0,1:T(8,128)}) async-done(((f32[1024,256]{1,0:T(8,128)}, f32[1024,1024]{0,1:T(8,128)}), (f32[1024,256]{1,0:T(8,128)}, f32[1024,1024]{0,1:T(8,128)})) %all-reduce.8.cloned.1.call-update) | async-done | bytes 5242896 | tf_op jit(solution)/shard_map/psum | solution.py:43
  331.9 5.5 copy.5
  337.5 4.4 fusion
  341.9 1.9 copy-done
  343.9 11.7 %cholesky.223 = f32[128,128]{1,0:T(8,128)S(1)} custom-call(f32[128,128]{1,0:T(8,128)S(1)} %cholesky.580), custom_call_target="Cholesky" | custom-call | tf_op jit(solution)/shard_map/jit(cholesky)/cholesky | solution.py:44
  355.6 2.5 cholesky.255
  358.1 9.8 %custom-call.63 = f32[1,128,128]{1,2,0:T(8,128)S(1)} custom-call(f32[1,128,128]{2,1,0:T(8,128)S(1)} %get-tuple-element.79), custom_call_target="InvertDiagBlocksLowerTriangular" | custom-call | tf_op jit(solution)/shard_map/jit(cholesky)/cholesky | solution.py:44
  367.9 2.4 constant_dynamic-update-slice_fusion.35
  370.3 1.5 convolution_subtract_fusion
  371.9 12.1 %cholesky.244 = f32[128,128]{1,0:T(8,128)S(1)} custom-call(f32[128,128]{1,0:T(8,128)S(1)} %cholesky.584), custom_call_target="Cholesky" | custom-call | tf_op jit(solution)/shard_map/jit(cholesky)/cholesky | solution.py:44
  384.6 9.8 %custom-call.64 = f32[1,128,128]{1,2,0:T(8,128)S(1)} custom-call(f32[1,128,128]{2,1,0:T(8,128)S(1)} %get-tuple-element.76), custom_call_target="InvertDiagBlocksLowerTriangular" | custom-call | tf_op jit(solution)/shard_map/jit(cholesky)/cholesky | solution.py:44
  395.7 2.1 convolution_subtract_fusion.1
  397.8 11.7 %cholesky.468 = f32[128,128]{1,0:T(8,128)S(1)} custom-call(f32[128,128]{1,0:T(8,128)S(1)} %cholesky.589), custom_call_target="Cholesky" | custom-call | tf_op jit(solution)/shard_map/jit(cholesky)/cholesky | solution.py:44
  410.8 9.8 %custom-call.65 = f32[1,128,128]{1,2,0:T(8,128)S(1)} custom-call(f32[1,128,128]{2,1,0:T(8,128)S(1)} %get-tuple-element.73), custom_call_target="InvertDiagBlocksLowerTriangular" | custom-call | tf_op jit(solution)/shard_map/jit(cholesky)/cholesky | solution.py:44
  421.8 2.3 convolution_subtract_fusion.2
  424.1 11.8 %cholesky.487 = f32[128,128]{1,0:T(8,128)S(1)} custom-call(f32[128,128]{1,0:T(8,128)S(1)} %cholesky.594), custom_call_target="Cholesky" | custom-call | tf_op jit(solution)/shard_map/jit(cholesky)/cholesky | solution.py:44
  437.3 9.8 %custom-call.66 = f32[1,128,128]{1,2,0:T(8,128)S(1)} custom-call(f32[1,128,128]{2,1,0:T(8,128)S(1)} %get-tuple-element.70), custom_call_target="InvertDiagBlocksLowerTriangular" | custom-call | tf_op jit(solution)/shard_map/jit(cholesky)/cholesky | solution.py:44
  448.3 2.3 convolution_subtract_fusion.3
  450.6 11.7 %cholesky.506 = f32[128,128]{1,0:T(8,128)S(1)} custom-call(f32[128,128]{1,0:T(8,128)S(1)} %cholesky.599), custom_call_target="Cholesky" | custom-call | tf_op jit(solution)/shard_map/jit(cholesky)/cholesky | solution.py:44
  463.7 10.0 %custom-call.67 = f32[1,128,128]{1,2,0:T(8,128)S(1)} custom-call(f32[1,128,128]{2,1,0:T(8,128)S(1)} %get-tuple-element.67), custom_call_target="InvertDiagBlocksLowerTriangular" | custom-call | tf_op jit(solution)/shard_map/jit(cholesky)/cholesky | solution.py:44
  474.7 2.3 convolution_subtract_fusion.4
  477.0 11.7 %cholesky.526 = f32[128,128]{1,0:T(8,128)S(1)} custom-call(f32[128,128]{1,0:T(8,128)S(1)} %cholesky.604), custom_call_target="Cholesky" | custom-call | tf_op jit(solution)/shard_map/jit(cholesky)/cholesky | solution.py:44
  490.0 9.8 %custom-call.68 = f32[1,128,128]{1,2,0:T(8,128)S(1)} custom-call(f32[1,128,128]{2,1,0:T(8,128)S(1)} %get-tuple-element.64), custom_call_target="InvertDiagBlocksLowerTriangular" | custom-call | tf_op jit(solution)/shard_map/jit(cholesky)/cholesky | solution.py:44
  500.8 2.0 convolution_subtract_fusion.11
  502.8 12.1 %cholesky.546 = f32[128,128]{1,0:T(8,128)S(1)} custom-call(f32[128,128]{1,0:T(8,128)S(1)} %cholesky.609), custom_call_target="Cholesky" | custom-call | tf_op jit(solution)/shard_map/jit(cholesky)/cholesky | solution.py:44
  516.3 9.8 %custom-call.69 = f32[1,128,128]{1,2,0:T(8,128)S(1)} custom-call(f32[1,128,128]{2,1,0:T(8,128)S(1)} %get-tuple-element.61), custom_call_target="InvertDiagBlocksLowerTriangular" | custom-call | tf_op jit(solution)/shard_map/jit(cholesky)/cholesky | solution.py:44
  526.9 1.8 convolution_subtract_fusion.13
  528.7 11.7 %cholesky.564 = f32[128,128]{1,0:T(8,128)S(1)} custom-call(f32[128,128]{1,0:T(8,128)S(1)} %convolution_subtract_fusion.13), custom_call_target="Cholesky" | custom-call | tf_op jit(solution)/shard_map/jit(cholesky)/cholesky | solution.py:44
  547.6 4.9 select_select_fusion
  552.4 22.8 %while.1 = (s32[]{:T(128)}, f32[1024,1024]{1,0:T(8,128)}, s32[8,2]{0,1:T(2,128)S(1)}, f32[8,128,128]{2,1,0:T(8,128)S(1)}, s32[]{:T(128)}) while((s32[]{:T(128)}, f32[1024,1024]{1,0:T(8,128)}, s32[8,2]{0,1:T(2,128)S(1)}, f32[8,128,128]{2,1,0:T(8,128)S(1)}, s32[]{:T(128)}) %tuple.63), condition=%wide.while_cond, body=%wide.while_body.sunk | while | flops 2 | bytes 131181 | solution.py:45
  553.1 2.2 bitcast_dynamic-update-slice_fusion.2
  555.9 2.2 bitcast_dynamic-update-slice_fusion.2
  558.8 2.2 bitcast_dynamic-update-slice_fusion.2
  561.6 2.2 bitcast_dynamic-update-slice_fusion.2
  564.5 2.2 bitcast_dynamic-update-slice_fusion.2
  567.4 2.2 bitcast_dynamic-update-slice_fusion.2
  570.2 2.2 bitcast_dynamic-update-slice_fusion.2
  573.1 2.2 bitcast_dynamic-update-slice_fusion.2
  575.3 78.8 %custom-call.70 = f32[8,128,128]{1,2,0:T(8,128)S(1)} custom-call(f32[8,128,128]{2,1,0:T(8,128)S(1)} %get-tuple-element.12), custom_call_target="InvertDiagBlocksLowerTriangular" | custom-call | tf_op jit(solution)/shard_map/jit(_solve_triangular)/triangular_solve | solution.py:45
  660.7 1.5 convolution_subtract_fusion.5
  662.5 1.5 convolution_subtract_fusion.9
  664.3 1.6 convolution_subtract_fusion.12
  (82 shorter events, 31.7 us)
Async XLA Ops:
  6.5 189.9 %all-reduce.6.cloned.1.call-start = ((), (), s32[]{:S(2)}) async-start(), calls=%async_computation | async-start | bytes 10485760 | tf_op jit(solution)/shard_map/psum | solution.py:13
  12.1 319.8 %all-reduce.8.cloned.1.call-start = ((), (), s32[]{:S(2)}) async-start(), calls=%async_computation.1 | async-start | bytes 10485760 | tf_op jit(solution)/shard_map/psum | solution.py:43
  196.5 3.2 copy-start.2
  196.5 3.4 copy-start.1
  200.1 18.7 %copy-start.3 = (f32[256,256]{1,0:T(8,128)S(1)}, f32[256,256]{1,0:T(8,128)}, u32[]{:S(2)}) copy-start(f32[256,256]{1,0:T(8,128)} %param.3) | copy-start | bytes 786436
  341.9 1.9 copy-start
  547.5 106.5 %copy-start.4 = (f32[1024,256]{1,0:T(8,128)S(1)}, f32[1024,256]{1,0:T(8,128)}, u32[]{:S(2)}) copy-start(f32[1024,256]{1,0:T(8,128)} %get-tuple-element.25) | copy-start | bytes 3145732
Sparse Core Ops, SparseCore 0:
  12.2 184.1 all-reduce.5
  228.5 103.4 all-reduce.7
where the time goes:
time: 684 us; the launch traced here: 674 us
  waiting for transfers between devices  288 us (42%)
  other arithmetic  267 us (39%)
  matrix products  63.4 us (9%)
  local copies, waits for them, and re-layouts  36.3 us (5%)
  between operations  19.2 us (3%)
    psum x1, waiting for transfers between devices, spread(): return lax.psum(kept, axis)  184 us
    another operation x30, other arithmetic, on_device(): lower = jnp.linalg.cholesky(gram)  173 us
    psum x1, waiting for transfers between devices, on_device(): lax.psum((inner_dot(panels, panels), inner_dot(panels, stacked)), 'row')  104 us
    another operation x3, other arithmetic, on_device(): factor = jax.scipy.linalg.solve_triangular(lower, cross, lower=True)  83.6 us
    dot_general x2, matrix products, inner_dot(): return jnp.dot(left.T, right, precision=lax.Precision.HIGHEST)  28.2 us
    another operation x14, matrix products, on_device(): lower = jnp.linalg.cholesky(gram)  23.1 us
    another operation x24, local copies, waits for them, and re-layouts  22.7 us
  transfers between devices with their start and end apart: 2, of which 2 were waited for; matrix products, arithmetic and copies ran while one was open for 0% of the time, Pallas kernels for 0%

commit v1 on v0

v1 whole, which is shorter than its diff:
```python
import functools

import jax
import jax.numpy as jnp
from jax import lax
from jax.experimental import pallas as pl
from jax.experimental.pallas import tpu as pltpu
from jax.sharding import Mesh
from jax.sharding import PartitionSpec as P

B = 256
P_SIZE = 4
ARC_ROWS = 128
NB = 128
SUB = 8
HIGHEST = lax.Precision.HIGHEST


def dot(left, right):
    return jnp.dot(left, right, precision=HIGHEST, preferred_element_type=jnp.float32)


def dot_t(left, right):
    return lax.dot_general(
        left, right, (((0,), (0,)), ((), ())), precision=HIGHEST, preferred_element_type=jnp.float32
    )


def inverse_factor(rows):
    n = NB // SUB
    tile = (SUB, NB)
    row_id = lax.broadcasted_iota(jnp.int32, tile, 0)
    col_id = lax.broadcasted_iota(jnp.int32, tile, 1)
    right = [jnp.where(row_id + r * SUB == col_id, 1.0, 0.0).astype(jnp.float32) for r in range(n)]
    for b in range(n):
        j = b * SUB
        head = rows[b]
        pivot = {}
        for k in range(SUB):
            for m in range(k, SUB):
                pivot[k, m] = jnp.broadcast_to(head[k : k + 1, j + m : j + m + 1], tile)
        scale = []
        for k in range(SUB):
            scale.append(lax.rsqrt(pivot[k, k]))
            for m in range(k + 1, SUB):
                pivot[k, m] = pivot[k, m] * scale[k]
            for m in range(k + 1, SUB):
                for q in range(m, SUB):
                    pivot[m, q] = pivot[m, q] - pivot[k, m] * pivot[k, q]
        top, top_right = [], []
        for k in range(SUB):
            here = jnp.broadcast_to(rows[b][k : k + 1, :], tile)
            there = jnp.broadcast_to(right[b][k : k + 1, :], tile)
            for m in range(k):
                here = here - pivot[m, k] * top[m]
                there = there - pivot[m, k] * top_right[m]
            top.append(here * scale[k])
            top_right.append(there * scale[k])
        strip = top_right[0]
        for k in range(1, SUB):
            strip = jnp.where(row_id == k, top_right[k], strip)
        for r in range(b + 1, n):
            left = []
            for k in range(SUB):
                part = jnp.broadcast_to(rows[r][:, j + k : j + k + 1], tile)
                for m in range(k):
                    part = part - pivot[m, k] * left[m]
                left.append(part * scale[k])
            body, body_right = rows[r], right[r]
            for k in range(SUB):
                body = body - left[k] * top[k]
                body_right = body_right - left[k] * top_right[k]
            rows[r], right[r] = body, body_right
        right[b] = strip
    return right


def factor_kernel(gram_ref, own_ref, out_ref, work, inv):
    lead = P_SIZE * B
    for c in range(P_SIZE):
        for r in range(c + 1):
            work[r * B : (r + 1) * B, c * B : (c + 1) * B] = gram_ref[c, r]
    work[:, lead:] = own_ref[...]
    steps = lead // NB

    def step(b, carry):
        start = pl.multiple_of(b * NB, NB)
        rows = [
            work[pl.ds(pl.multiple_of(start + r * SUB, SUB), SUB), pl.ds(start, NB)]
            for r in range(NB // SUB)
        ]
        right = inverse_factor(rows)
        for r in range(NB // SUB):
            inv[r * SUB : (r + 1) * SUB, :] = right[r]
        for s in range(steps):

            @pl.when(b == s)
            def _(s=s):
                lo, hi = s * NB, (s + 1) * NB
                panel = dot(inv[...], work[lo:hi, lo:])
                out_ref[lo:hi, :] = panel[:, lead - lo :]
                for i in range(s + 1, steps):
                    at = i * NB
                    off = at - lo
                    work[at : at + NB, at:] = work[at : at + NB, at:] - dot_t(
                        panel[:, off : off + NB], panel[:, off:]
                    )

        return carry

    lax.fori_loop(0, steps, step, 0)


def factor_columns(gram, own):
    lead = P_SIZE * B
    columns = own.shape[1]
    return pl.pallas_call(
        factor_kernel,
        out_shape=jax.ShapeDtypeStruct((lead, columns), jnp.float32),
        in_specs=[pl.BlockSpec(memory_space=pltpu.VMEM)] * 2,
        out_specs=pl.BlockSpec(memory_space=pltpu.VMEM),
        scratch_shapes=[
            pltpu.VMEM((lead, lead + columns), jnp.float32),
            pltpu.VMEM((NB, NB), jnp.float32),
        ],
        compiler_params=pltpu.CompilerParams(vmem_limit_bytes=40 * 1024 * 1024),
        name="factor_columns",
    )(gram, own)


def from_first(value, n_hi):
    at = lax.axis_index("hi")
    have = 1
    while have < n_hi:
        more = min(have, n_hi - have)
        got = lax.ppermute(value, "hi", [(g, g + have) for g in range(more)])
        value = jnp.where(at < have, value, got)
        have += more
    return value


def on_device(r_slab, arc_rows, arc_blocks):
    n_hi = lax.axis_size("hi")
    col_index = lax.axis_index("hi") * P_SIZE + lax.axis_index("lo")
    row_index = lax.axis_index("row")
    n_arcs, blocks_here = arc_blocks.shape
    live = arc_blocks.astype(jnp.float32)
    masked = (arc_rows.reshape(n_arcs, ARC_ROWS, blocks_here, B) * live[:, None, :, None]).reshape(
        arc_rows.shape
    )
    stacked = jnp.concatenate([r_slab, masked], axis=0)
    panels = lax.all_gather(from_first(stacked, n_hi), "lo")
    cross = jnp.einsum("lkm,kn->lmn", panels, stacked, precision=HIGHEST)
    mine = lax.psum_scatter(cross, "row", scatter_dimension=0, tiled=True)
    own = lax.all_gather(mine, "row", axis=0, tiled=True).reshape(P_SIZE * B, B)
    gram = lax.all_gather(from_first(mine, n_hi), ("lo", "row"), axis=0, tiled=True)
    gram = gram.reshape(P_SIZE, P_SIZE, B, B)
    factor = factor_columns(gram, own)
    result = lax.dynamic_slice_in_dim(factor, row_index * B, B, 0)
    row_ids = row_index * B + lax.broadcasted_iota(jnp.int32, result.shape, 0)
    col_ids = col_index * B + lax.broadcasted_iota(jnp.int32, result.shape, 1)
    return jnp.where(col_ids >= row_ids, result, jnp.zeros_like(result))


def solution(mesh):
    n_col, n_row = mesh.shape["col"], mesh.shape["row"]
    split = Mesh(
        mesh.devices.reshape(n_col // P_SIZE, P_SIZE, n_row),
        ("hi", "lo", "row"),
    )
    spec = P("row", ("hi", "lo"))
    return jax.shard_map(
        on_device,
        mesh=split,
        in_specs=(spec, spec, spec),
        out_specs=spec,
        check_vma=False,
    )
```

time: 684 us -> 318 us (0.46); the launches traced: 674 us -> 316 us
  other arithmetic: 267 us -> 7.05 us
  waiting for transfers between devices: 288 us -> 227 us
  matrix products: 63.4 us -> 11.8 us
  Pallas kernels: 0 us -> 44.6 us
  local copies, waits for them, and re-layouts: 36.3 us -> 3.49 us
  starting transfers between devices: 0.04 us -> 8.45 us
    psum x2 -> x0, waiting for transfers between devices: 288 us -> none  [the longest x1 184 us: spread(): return lax.psum(kept, axis)]
    another operation x33 -> x0, other arithmetic: 256 us -> none  [the longest x30 173 us: on_device(): lower = jnp.linalg.cholesky(gram)]
    all_gather x0 -> x3, waiting for transfers between devices: none -> 134 us  [the longest x1 97.3 us: on_device(): panels = lax.all_gather(from_first(stacked, n_hi), 'lo')]
    ppermute x0 -> x2, waiting for transfers between devices: none -> 68.6 us  [from_first(): got = lax.ppermute(value, 'hi', [(g, g + have) for g in range(more)])]
    pallas_call x0 -> x1, Pallas kernels: none -> 44.6 us  [factor_columns(): pl.pallas_call(factor_kernel, out_shape=jax.ShapeDtypeStruct((lead, colum...]
    another operation x29 -> x0, matrix products: 35.2 us -> none  [the longest x14 23.1 us: on_device(): lower = jnp.linalg.cholesky(gram)]
    another operation x33 -> x0, local copies, waits for them, and re-layouts: 25.2 us -> none
    reduce_scatter x0 -> x1, waiting for transfers between devices: none -> 24.8 us  [on_device(): mine = lax.psum_scatter(cross, 'row', scatter_dimension=0, tiled=True)]
  transfers between devices with their start and end apart: 2 -> 6, of which waited for: 2 -> 6; matrix products, arithmetic and copies ran while one was open for 0% -> 1% of each run, Pallas kernels for 0% -> 0%
where the time goes in v1:
time: 318 us; the launch traced here: 316 us
  waiting for transfers between devices  227 us (71%)
  Pallas kernels  44.6 us (14%)
  between operations  13.2 us (4%)
  matrix products  11.8 us (4%)
  starting transfers between devices  8.45 us (3%)
  other arithmetic  7.05 us (2%)
  local copies, waits for them, and re-layouts  3.49 us (1%)
    all_gather x1, waiting for transfers between devices, on_device(): panels = lax.all_gather(from_first(stacked, n_hi), 'lo')  97.3 us
    ppermute x2, waiting for transfers between devices, from_first(): got = lax.ppermute(value, 'hi', [(g, g + have) for g in range(more)])  68.6 us
    pallas_call x1, Pallas kernels, factor_columns(): pl.pallas_call(factor_kernel, out_shape=jax.ShapeDtypeStruct((lead, colum...  44.6 us
    all_gather x1, waiting for transfers between devices, on_device(): lax.all_gather(from_first(mine, n_hi), ('lo', 'row'), axis=0, tiled=True)  35.6 us
    reduce_scatter x1, waiting for transfers between devices, on_device(): mine = lax.psum_scatter(cross, 'row', scatter_dimension=0, tiled=True)  24.8 us
    dot_general x1, matrix products, on_device(): cross = jnp.einsum('lkm,kn->lmn', panels, stacked, precision=HIGHEST)  11.8 us
    ppermute x2, starting transfers between devices, from_first(): got = lax.ppermute(value, 'hi', [(g, g + have) for g in range(more)])  8.33 us
  transfers between devices with their start and end apart: 6, of which 6 were waited for; matrix products, arithmetic and copies ran while one was open for 1% of the time, Pallas kernels for 0%

profile of v1, /device:TPU:9, one launch (start us, length us, event | category | flops | bytes accessed | tf_op | source)
XLA Modules:
  0.0 316.0 jit_solution(16121428407686728748)
XLA Ops:
  6.5 0.0 copy-start.2
  6.5 0.0 all-gather.9.cloned.1.call-start
  6.5 0.7 convert_bitcast_fusion
  7.2 0.1 broadcast_bitcast_fusion
  7.3 1.4 broadcast_multiply_fusion
  8.7 0.0 copy-done.2
  8.8 1.2 pad_maximum_fusion
  9.9 4.3 %collective-permute-start = (f32[1280,256]{1,0:T(8,128)}, f32[1280,256]{1,0:T(8,128)S(1)}, u32[]{:S(2)}, u32[]{:S(2)}) collective-permute-start(f32[1280,256]{1,0:T(8,128)} %pad_maximum_fusion), channel_id=1, source_target_pairs={{0,16},{1,17},{2,18},{3,19},{4,20},{5,21},{6,22},{7,23},{8,24},{9,... | collective-permute-start | bytes 3932168 | tf_op jit(solution)/shard_map/ppermute | solution.py:136
  14.2 56.7 %collective-permute-done = f32[1280,256]{1,0:T(8,128)S(1)} collective-permute-done((f32[1280,256]{1,0:T(8,128)}, f32[1280,256]{1,0:T(8,128)S(1)}, u32[]{:S(2)}, u32[]{:S(2)}) %collective-permute-start) | collective-permute-done | bytes 1310752 | tf_op jit(solution)/shard_map/ppermute | solution.py:136
  70.9 1.3 broadcast_select_fusion
  72.2 0.0 all-gather.9.cloned.1.call-update
  72.2 0.0 reduce-scatter.2.cloned.1.call-start
  72.2 97.3 %all-gather.9.cloned.1.call-done = f32[5120,256]{1,0:T(8,128)} async-done(((f32[1280,256]{1,0:T(8,128)}), f32[5120,256]{1,0:T(8,128)}) %all-gather.9.cloned.1.call-update) | async-done | bytes 5242896 | tf_op jit(solution)/shard_map/all_gather | solution.py:152
  169.5 11.8 %fusion = f32[4,256,256]{2,1,0:T(8,128)} fusion(f32[4,1280,256]{2,1,0:T(8,128)} %bitcast.13, f32[1024,256]{1,0:T(8,128)S(1)} %broadcast_multiply_fusion, f32[256,256]{1,0:T(8,128)S(1)} %copy-done.2), kind=kOutput, calls=%fused_computation.1 | convolution fusion | flops 4026859520 | bytes 7602176 | tf_op jit(solution)/shard_map/lkm,kn->lmn/dot_general | solution.py:153
  181.3 0.0 reduce-scatter.2.cloned.1.call-update
  181.3 0.0 all-gather.7.cloned.1.call-start
  181.4 24.8 %reduce-scatter.2.cloned.1.call-done = f32[1,256,256]{2,1,0:T(8,128)} async-done(((f32[4,256,256]{2,1,0:T(8,128)}), f32[1,256,256]{2,1,0:T(8,128)}) %reduce-scatter.2.cloned.1.call-update) | async-done | bytes 262160 | tf_op jit(solution)/shard_map/reduce_scatter | solution.py:154
  206.2 0.0 all-gather.7.cloned.1.call-update
  206.2 0.0 all-gather.5.cloned.1.call-start
  206.3 4.0 %collective-permute-start.1 = (f32[1,256,256]{2,1,0:T(8,128)}, f32[1,256,256]{2,1,0:T(8,128)S(1)}, u32[]{:S(2)}, u32[]{:S(2)}) collective-permute-start(f32[1,256,256]{2,1,0:T(8,128)} %reduce-scatter.2.cloned.1.call-done), channel_id=1, source_target_pairs={{0,16},{1,17},{2,18},{3,19},{4,20},{5,21},{6,22},{7,23},{8,24},{9,... | collective-permute-start | bytes 786440 | tf_op jit(solution)/shard_map/ppermute | solution.py:136
  210.3 11.9 %collective-permute-done.1 = f32[1,256,256]{2,1,0:T(8,128)S(1)} collective-permute-done((f32[1,256,256]{2,1,0:T(8,128)}, f32[1,256,256]{2,1,0:T(8,128)S(1)}, u32[]{:S(2)}, u32[]{:S(2)}) %collective-permute-start.1) | collective-permute-done | bytes 262176 | tf_op jit(solution)/shard_map/ppermute | solution.py:136
  222.2 1.7 broadcast_select_fusion.1
  223.9 0.0 all-gather.5.cloned.1.call-update
  223.9 1.1 all-gather.7.cloned.1.call-done
  225.0 35.6 %all-gather.5.cloned.1.call-done = f32[16,256,256]{2,1,0:T(8,128)} async-done(((f32[1,256,256]{2,1,0:T(8,128)}), f32[16,256,256]{2,1,0:T(8,128)}) %all-gather.5.cloned.1.call-update) | async-done | bytes 4194320 | tf_op jit(solution)/shard_map/all_gather | solution.py:156
  260.6 0.0 copy-start
  260.6 2.2 copy-done
  262.8 0.0 copy-start.1
  262.8 1.2 copy-done.1
  264.0 44.6 %factor_columns.1 = f32[1024,256]{1,0:T(8,128)S(1)} custom-call(f32[4,4,256,256]{3,2,1,0:T(8,128)S(1)} %bitcast.11, f32[1024,256]{1,0:T(8,128)S(1)} %bitcast.12), custom_call_target="tpu_custom_call" | custom-call | tf_op jit(solution)/shard_map/factor_columns/pallas_call | solution.py:117
  308.7 0.8 dynamic-slice_select_fusion
  (1 shorter events, 0.0 us)
Async XLA Ops:
  6.5 2.2 copy-start.2
  6.5 163.0 %all-gather.9.cloned.1.call-start = ((), (), s32[]{:S(2)}) async-start(), calls=%async_computation.4 | async-start | bytes 6553600 | tf_op jit(solution)/shard_map/all_gather | solution.py:152
  9.9 61.0 %collective-permute-start = (f32[1280,256]{1,0:T(8,128)}, f32[1280,256]{1,0:T(8,128)S(1)}, u32[]{:S(2)}, u32[]{:S(2)}) collective-permute-start(f32[1280,256]{1,0:T(8,128)} %pad_maximum_fusion), channel_id=1, source_target_pairs={{0,16},{1,17},{2,18},{3,19},{4,20},{5,21},{6,22},{7,23},{8,24},{9,... | collective-permute-start | bytes 3932168 | tf_op jit(solution)/shard_map/ppermute | solution.py:136
  72.2 134.0 %reduce-scatter.2.cloned.1.call-start = ((), (), s32[]{:S(2)}) async-start(), calls=%async_computation.1 | async-start | bytes 1310720 | tf_op jit(solution)/shard_map/reduce_scatter | solution.py:154
  181.3 43.7 %all-gather.7.cloned.1.call-start = ((), (), s32[]{:S(2)}) async-start(), calls=%async_computation.3 | async-start | bytes 1310720 | tf_op jit(solution)/shard_map/all_gather | solution.py:155
  206.2 54.4 %all-gather.5.cloned.1.call-start = ((), (), s32[]{:S(2)}) async-start(), calls=%async_computation.2 | async-start | bytes 4456448 | tf_op jit(solution)/shard_map/all_gather | solution.py:156
  206.3 15.9 %collective-permute-start.1 = (f32[1,256,256]{2,1,0:T(8,128)}, f32[1,256,256]{2,1,0:T(8,128)S(1)}, u32[]{:S(2)}, u32[]{:S(2)}) collective-permute-start(f32[1,256,256]{2,1,0:T(8,128)} %reduce-scatter.2.cloned.1.call-done), channel_id=1, source_target_pairs={{0,16},{1,17},{2,18},{3,19},{4,20},{5,21},{6,22},{7,23},{8,24},{9,... | collective-permute-start | bytes 786440 | tf_op jit(solution)/shard_map/ppermute | solution.py:136
  260.6 2.2 copy-start
  262.8 1.2 copy-start.1
Sparse Core Ops, SparseCore 0:
  72.3 97.1 all-gather.8
  181.5 24.6 reduce-scatter.1
  207.8 17.1 all-gather.6
  226.5 34.0 all-gather.4

commit v2 on v1

--- a/solution.py
+++ b/solution.py
@@ -1,5 +1,3 @@
-import functools
-
 import jax
 import jax.numpy as jnp
 from jax import lax
@@ -75,11 +73,35 @@
     return right
 
 
+PAIRS = [(r, c) for r in range(P_SIZE) for c in range(r, P_SIZE)]
+
+
+def upper_products_kernel(rows_ref, out_ref):
+    for at, (r, c) in enumerate(PAIRS):
+        out_ref[at] = dot_t(rows_ref[r], rows_ref[c])
+
+
+def all_products_kernel(left_ref, right_ref, out_ref):
+    for c in range(P_SIZE):
+        for r in range(P_SIZE):
+            out_ref[c, r] = dot_t(left_ref[r], right_ref[c])
+
+
+def on_chip(kernel, shape, name, *operands):
+    return pl.pallas_call(
+        kernel,
+        out_shape=jax.ShapeDtypeStruct(shape, jnp.float32),
+        in_specs=[pl.BlockSpec(memory_space=pltpu.VMEM)] * len(operands),
+        out_specs=pl.BlockSpec(memory_space=pltpu.VMEM),
+        compiler_params=pltpu.CompilerParams(vmem_limit_bytes=32 * 1024 * 1024),
+        name=name,
+    )(*operands)
+
+
 def factor_kernel(gram_ref, own_ref, out_ref, work, inv):
     lead = P_SIZE * B
-    for c in range(P_SIZE):
-        for r in range(c + 1):
-            work[r * B : (r + 1) * B, c * B : (c + 1) * B] = gram_ref[c, r]
+    for at, (r, c) in enumerate(PAIRS):
+        work[r * B : (r + 1) * B, c * B : (c + 1) * B] = gram_ref[at]
     work[:, lead:] = own_ref[...]
     steps = lead // NB
 
@@ -144,17 +166,23 @@
     col_index = lax.axis_index("hi") * P_SIZE + lax.axis_index("lo")
     row_index = lax.axis_index("row")
     n_arcs, blocks_here = arc_blocks.shape
+    columns = arc_rows.shape[1]
     live = arc_blocks.astype(jnp.float32)
     masked = (arc_rows.reshape(n_arcs, ARC_ROWS, blocks_here, B) * live[:, None, :, None]).reshape(
         arc_rows.shape
     )
     stacked = jnp.concatenate([r_slab, masked], axis=0)
-    panels = lax.all_gather(from_first(stacked, n_hi), "lo")
-    cross = jnp.einsum("lkm,kn->lmn", panels, stacked, precision=HIGHEST)
-    mine = lax.psum_scatter(cross, "row", scatter_dimension=0, tiled=True)
-    own = lax.all_gather(mine, "row", axis=0, tiled=True).reshape(P_SIZE * B, B)
-    gram = lax.all_gather(from_first(mine, n_hi), ("lo", "row"), axis=0, tiled=True)
-    gram = gram.reshape(P_SIZE, P_SIZE, B, B)
+    quarters = stacked.reshape(P_SIZE, stacked.shape[0] // P_SIZE, columns)
+    quarters = lax.all_to_all(quarters, "lo", 0, 0)
+    group = ("lo", "row")
+    gram = on_chip(upper_products_kernel, (len(PAIRS), B, B), "upper_products", quarters)
+    gram = lax.psum_scatter(gram.reshape(-1, B), group, scatter_dimension=0, tiled=True)
+    gram = lax.all_gather(from_first(gram, n_hi), group, axis=0, tiled=True)
+    gram = gram.reshape(len(PAIRS), B, B)
+    panels = from_first(quarters, n_hi)
+    cross = on_chip(all_products_kernel, (P_SIZE, P_SIZE, B, B), "all_products", panels, quarters)
+    mine = lax.psum_scatter(cross.reshape(-1, B), group, scatter_dimension=0, tiled=True)
+    own = lax.all_gather(mine, "row", axis=0, tiled=True)
     factor = factor_columns(gram, own)
     result = lax.dynamic_slice_in_dim(factor, row_index * B, B, 0)
     row_ids = row_index * B + lax.broadcasted_iota(jnp.int32, result.shape, 0)

time: 318 us -> 284 us (0.89)
  waiting for transfers between devices: 227 us -> 170 us
  blocking collectives: 0 us -> 18.7 us
  matrix products: 11.8 us -> 0 us
  Pallas kernels: 44.6 us -> 56 us
  starting transfers between devices: 8.45 us -> 13.1 us
    all_gather x3 -> x2, waiting for transfers between devices: 134 us -> 53.2 us  [the longest x1 35 us: on_device(): gram = lax.all_gather(from_first(gram, n_hi), group, axis=0, tiled=True)]
    reduce_scatter x1 -> x2, waiting for transfers between devices: 24.8 us -> 58.3 us  [the longest x1 58.3 us: on_device(): lax.psum_scatter(cross.reshape(-1, B), group, scatter_dimension=0, tiled=...]
    all_to_all x0 -> x1, blocking collectives: none -> 18.7 us  [on_device(): quarters = lax.all_to_all(quarters, 'lo', 0, 0)]
    dot_general x1 -> x0, matrix products: 11.8 us -> none  [on_device(): cross = jnp.einsum('lkm,kn->lmn', panels, stacked, precision=HIGHEST)]
    pallas_call x0 -> x2, Pallas kernels: none -> 11.4 us  [on_chip(): pl.pallas_call(kernel, out_shape=jax.ShapeDtypeStruct(shape, jnp.float32)...]
    ppermute x2, waiting for transfers between devices: 68.6 us -> 58.9 us  [from_first(): got = lax.ppermute(value, 'hi', [(g, g + have) for g in range(more)])]
    ppermute x2, starting transfers between devices: 8.33 us -> 13 us  [from_first(): got = lax.ppermute(value, 'hi', [(g, g + have) for g in range(more)])]
    unnamed x6 -> x10, local copies, waits for them, and re-layouts: 3.42 us -> 6.43 us
  transfers between devices with their start and end apart: 6 -> 6, of which waited for: 6 -> 5; matrix products, arithmetic and copies ran while one was open for 1% -> 1% of each run, Pallas kernels for 0% -> 2%
where the time goes in v2:
time: 284 us; the launch traced here: 283 us
  waiting for transfers between devices  170 us (60%)
  Pallas kernels  56 us (20%)
  blocking collectives  18.7 us (7%)
  between operations  13.2 us (5%)
  starting transfers between devices  13.1 us (5%)
  local copies, waits for them, and re-layouts  6.5 us (2%)
  other arithmetic  4.8 us (2%)
    ppermute x2, waiting for transfers between devices, from_first(): got = lax.ppermute(value, 'hi', [(g, g + have) for g in range(more)])  58.9 us
    reduce_scatter x1, waiting for transfers between devices, on_device(): lax.psum_scatter(cross.reshape(-1, B), group, scatter_dimension=0, tiled=...  58.3 us
    pallas_call x1, Pallas kernels, factor_columns(): pl.pallas_call(factor_kernel, out_shape=jax.ShapeDtypeStruct((lead, colum...  44.6 us
    all_gather x1, waiting for transfers between devices, on_device(): gram = lax.all_gather(from_first(gram, n_hi), group, axis=0, tiled=True)  35 us
    all_to_all x1, blocking collectives, on_device(): quarters = lax.all_to_all(quarters, 'lo', 0, 0)  18.7 us
    all_gather x1, waiting for transfers between devices, on_device(): own = lax.all_gather(mine, 'row', axis=0, tiled=True)  18.2 us
    ppermute x2, starting transfers between devices, from_first(): got = lax.ppermute(value, 'hi', [(g, g + have) for g in range(more)])  13 us
    pallas_call x2, Pallas kernels, on_chip(): pl.pallas_call(kernel, out_shape=jax.ShapeDtypeStruct(shape, jnp.float32)...  11.4 us
  transfers between devices with their start and end apart: 6, of which 5 were waited for; matrix products, arithmetic and copies ran while one was open for 1% of the time, Pallas kernels for 2%

profile of v2, /device:TPU:9, one launch (start us, length us, event | category | flops | bytes accessed | tf_op | source)
XLA Modules:
  0.0 282.9 jit_solution(9642469277271399896)
XLA Ops:
  6.5 0.0 copy-start.4
  6.5 0.0 reduce-scatter.3.cloned.1.call-start
  6.5 0.7 convert_bitcast_fusion
  7.2 0.1 broadcast_bitcast_fusion
  7.3 1.4 broadcast_multiply_fusion
  8.7 0.0 copy-done.4
  8.8 0.1 pad_maximum_fusion
  8.8 18.7 %all_to_all.5.rows_ref.right_ref = f32[4,320,256]{2,1,0:T(8,128)S(1)} all-to-all(f32[4,320,256]{2,1,0:T(8,128)S(1)} %bitcast.11), channel_id=1, replica_groups=mesh['hi'=2,'lo'=4,'row'=4] {'lo'}, dimensions={0} | all-to-all | bytes 2621440 | tf_op jit(solution)/shard_map/all_to_all | solution.py:176
  27.6 4.5 %upper_products.1 = f32[10,256,256]{2,1,0:T(8,128)S(1)} custom-call(f32[4,320,256]{2,1,0:T(8,128)S(1)} %all_to_all.5.rows_ref.right_ref), custom_call_target="tpu_custom_call" | custom-call | tf_op jit(solution)/shard_map/upper_products/pallas_call | solution.py:91
  32.1 0.0 copy-start.1
  32.1 1.5 copy-done.1
  33.6 0.0 reduce-scatter.3.cloned.1.call-update
  33.7 0.0 reduce-scatter.5.cloned.1.call-start
  33.7 4.3 %collective-permute-start.1 = (f32[4,320,256]{2,1,0:T(8,128)S(1)}, f32[4,320,256]{2,1,0:T(8,128)S(1)}, u32[]{:S(2)}, u32[]{:S(2)}) collective-permute-start(f32[4,320,256]{2,1,0:T(8,128)S(1)} %all_to_all.5.rows_ref.right_ref), channel_id=1, source_target_pairs={{0,16},{1,17},{2,18},{3,19},{4,20},{5,21},{6,22},{7,23},{8,24},{9,... | collective-permute-start | bytes 3932168 | tf_op jit(solution)/shard_map/ppermute | solution.py:158
  38.0 56.3 %collective-permute-done.1 = f32[4,320,256]{2,1,0:T(8,128)S(1)} collective-permute-done((f32[4,320,256]{2,1,0:T(8,128)S(1)}, f32[4,320,256]{2,1,0:T(8,128)S(1)}, u32[]{:S(2)}, u32[]{:S(2)}) %collective-permute-start.1) | collective-permute-done | bytes 1310752 | tf_op jit(solution)/shard_map/ppermute | solution.py:158
  94.4 0.2 broadcast_select_fusion.left_ref
  94.5 6.9 %all_products.1 = f32[4,4,256,256]{3,2,1,0:T(8,128)S(1)} custom-call(f32[4,320,256]{2,1,0:T(8,128)S(1)} %broadcast_select_fusion.left_ref, f32[4,320,256]{2,1,0:T(8,128)S(1)} %all_to_all.5.rows_ref.right_ref), custom_call_target="tpu_custom_call" | custom-call | tf_op jit(solution)/shard_map/all_products/pallas_call | solution.py:91
  101.4 0.0 copy-start
  101.4 1.9 copy-done
  103.4 0.0 reduce-scatter.5.cloned.1.call-update
  103.4 0.0 all-gather.3.cloned.1.call-start
  103.5 0.0 reduce-scatter.3.cloned.1.call-done
  103.5 8.7 %collective-permute-start = (f32[160,256]{1,0:T(8,128)}, f32[160,256]{1,0:T(8,128)S(1)}, u32[]{:S(2)}, u32[]{:S(2)}) collective-permute-start(f32[160,256]{1,0:T(8,128)} %reduce-scatter.3.cloned.1.call-done), channel_id=1, source_target_pairs={{0,16},{1,17},{2,18},{3,19},{4,20},{5,21},{6,22},{7,23},{8,24},{9,... | collective-permute-start | bytes 491528 | tf_op jit(solution)/shard_map/ppermute | solution.py:158
  112.2 2.6 collective-permute-done
  114.7 1.6 broadcast_select_fusion.1
  116.3 0.0 all-gather.3.cloned.1.call-update
  116.3 0.0 all-gather.5.cloned.1.call-start
  116.4 58.3 %reduce-scatter.5.cloned.1.call-done = f32[256,256]{1,0:T(8,128)} async-done(((f32[4096,256]{1,0:T(8,128)}), f32[256,256]{1,0:T(8,128)}) %reduce-scatter.5.cloned.1.call-update) | async-done | bytes 262160 | tf_op jit(solution)/shard_map/reduce_scatter | solution.py:184
  174.7 0.0 all-gather.5.cloned.1.call-update
  174.7 35.0 %all-gather.3.cloned.1.call-done = f32[2560,256]{1,0:T(8,128)} async-done(((f32[160,256]{1,0:T(8,128)}), f32[2560,256]{1,0:T(8,128)}) %all-gather.3.cloned.1.call-update) | async-done | bytes 2621456 | tf_op jit(solution)/shard_map/all_gather | solution.py:180
  209.7 18.2 %all-gather.5.cloned.1.call-done.own_ref = f32[1024,256]{1,0:T(8,128)} async-done(((f32[256,256]{1,0:T(8,128)}), f32[1024,256]{1,0:T(8,128)}) %all-gather.5.cloned.1.call-update) | async-done | bytes 1048592 | tf_op jit(solution)/shard_map/all_gather | solution.py:185
  227.9 0.0 copy-start.2
  227.9 1.7 copy-done.2
  229.7 0.0 copy-start.3
  229.7 1.2 copy-done.3
  230.9 44.6 %factor_columns.1 = f32[1024,256]{1,0:T(8,128)S(1)} custom-call(f32[10,256,256]{2,1,0:T(8,128)S(1)} %bitcast.10, f32[1024,256]{1,0:T(8,128)S(1)} %copy-done.3), custom_call_target="tpu_custom_call" | custom-call | tf_op jit(solution)/shard_map/factor_columns/pallas_call | solution.py:139
  275.5 0.8 dynamic-slice_select_fusion
  (1 shorter events, 0.0 us)
Async XLA Ops:
  6.5 2.2 copy-start.4
  6.5 96.9 %reduce-scatter.3.cloned.1.call-start = ((), (), s32[]{:S(2)}) async-start(), calls=%async_computation.3 | async-start | bytes 2785280 | tf_op jit(solution)/shard_map/reduce_scatter | solution.py:179
  32.1 1.5 copy-start.1
  33.7 141.0 %reduce-scatter.5.cloned.1.call-start = ((), (), s32[]{:S(2)}) async-start(), calls=%async_computation.5 | async-start | bytes 4456448 | tf_op jit(solution)/shard_map/reduce_scatter | solution.py:184
  33.7 60.6 %collective-permute-start.1 = (f32[4,320,256]{2,1,0:T(8,128)S(1)}, f32[4,320,256]{2,1,0:T(8,128)S(1)}, u32[]{:S(2)}, u32[]{:S(2)}) collective-permute-start(f32[4,320,256]{2,1,0:T(8,128)S(1)} %all_to_all.5.rows_ref.right_ref), channel_id=1, source_target_pairs={{0,16},{1,17},{2,18},{3,19},{4,20},{5,21},{6,22},{7,23},{8,24},{9,... | collective-permute-start | bytes 3932168 | tf_op jit(solution)/shard_map/ppermute | solution.py:158
  101.4 1.9 copy-start
  103.4 106.3 %all-gather.3.cloned.1.call-start = ((), (), s32[]{:S(2)}) async-start(), calls=%async_computation.4 | async-start | bytes 2785280 | tf_op jit(solution)/shard_map/all_gather | solution.py:180
  103.5 11.2 %collective-permute-start = (f32[160,256]{1,0:T(8,128)}, f32[160,256]{1,0:T(8,128)S(1)}, u32[]{:S(2)}, u32[]{:S(2)}) collective-permute-start(f32[160,256]{1,0:T(8,128)} %reduce-scatter.3.cloned.1.call-done), channel_id=1, source_target_pairs={{0,16},{1,17},{2,18},{3,19},{4,20},{5,21},{6,22},{7,23},{8,24},{9,... | collective-permute-start | bytes 491528 | tf_op jit(solution)/shard_map/ppermute | solution.py:158
  116.3 111.6 %all-gather.5.cloned.1.call-start = ((), (), s32[]{:S(2)}) async-start(), calls=%async_computation.6 | async-start | bytes 1310720 | tf_op jit(solution)/shard_map/all_gather | solution.py:185
  227.9 1.7 copy-start.2
  229.7 1.2 copy-start.3
Sparse Core Ops, SparseCore 0:
  33.8 60.6 reduce-scatter.2
  103.5 71.1 reduce-scatter.4
  176.3 33.3 all-gather.2
  211.1 16.7 all-gather.4
